TPU v7x, 32 devices: a whole 2x2x4 slice. The times are simulated.
32 devices in a mesh: dp: 4 (over z), seq: 8 (over y, x, core).
Axes of the slice: x: 2, y: 2, z: 4, core: 2. Of those that a mesh axis runs over, the one named last changes fastest.
Arguments:
- hidden: bfloat16 [4, 2048, 1024], P('dp', 'seq'), may hold values from -6 to 6
- segment_ids: int32 [4, 2048], P('dp'), may hold values from 0 to 31, never falling along the last dimension, each value on 1 to 512 neighbouring positions
- kernel: float32 [31, 1024], replicated, may hold values from -1 to 1
- norm_gain: float32 [1024], replicated, may hold values from 0.5 to 1.5
- projection: bfloat16 [1024, 1024], replicated, may hold values from -0.1875 to 0.1875
- cotangent: bfloat16 [4, 2048, 1024], P('dp', 'seq'), may hold values from -6 to 6
Outputs:
- conv_out: bfloat16 [4, 2048, 1024], P('dp', 'seq')
- grad_hidden: bfloat16 [4, 2048, 1024], P('dp', 'seq')
- grad_projection: float32 [1024, 1024], P('seq')
- grad_kernel: float32 [1024, 31], P('seq')
- grad_gain: float32 [1024], P('seq')
Inputs may be any that keep to these rules, and one draw needn't show every extreme that they name: `segment_ids`: within a row utterance numbers never fall, every number 0 to 31 occurs, each utterance spans 1 to 512 frames and one spans exactly 512.
All inputs are finite; a program needn't handle non-finite values.
Results may differ from a plain program's by a relative error of at most 0.005.
Values may be sent and summed in bfloat16 or wider, within the bound.
A program may use at most 64 MiB of HBM per device.

v0:
```python
import math

import jax
import jax.numpy as jnp
from jax import lax
from jax.sharding import PartitionSpec as P

EPS = 1e-05


def padded_2(value, sides, width):
    for axis, dim in sides:
        count, length = (lax.axis_size(axis), value.shape[dim])
        up = [(i, (i + 1) % count) for i in range(count - 1)]
        down = [(j, i) for i, j in up]
        last = lax.slice_in_dim(value, length - width, length, axis=dim)
        first = lax.slice_in_dim(value, 0, width, axis=dim)
        before = lax.ppermute(last, axis, up)
        after = lax.ppermute(first, axis, down)
        value = jnp.concatenate([before, value, after], axis=dim)
    return value


def from_behind(value, axis, steps):
    count = lax.axis_size(axis)
    first, last = (max(0, -steps), min(count, count - steps))
    return lax.ppermute(value, axis, [(source, source + steps) for source in range(first, last)])


def depth_forward(padded, segs, kernel, length):
    reach = kernel.shape[0] // 2
    total = jnp.zeros((length, kernel.shape[1]), jnp.float32)
    centre = segs[reach : reach + length]
    for offset in range(kernel.shape[0]):
        same = (segs[offset : offset + length] == centre).astype(jnp.float32)[:, None]
        total = total + kernel[offset] * padded[offset : offset + length].astype(jnp.float32) * same
    return total


def kernel_terms(grad, padded, segs, length, taps):
    reach = taps // 2
    centre = segs[reach : reach + length]
    rows_out = []
    for offset in range(taps):
        same = (segs[offset : offset + length] == centre).astype(jnp.float32)[:, None]
        rows_out.append(
            jnp.sum(grad * padded[offset : offset + length].astype(jnp.float32) * same, 0)
        )
    return jnp.stack(rows_out, 0)


def spread_back(grid, segs, kernel, length):
    reach = kernel.shape[0] // 2
    total = jnp.zeros((length, kernel.shape[1]), jnp.float32)
    centre = segs[reach : reach + length]
    for offset in range(kernel.shape[0]):
        lower = 2 * reach - offset
        same = (segs[lower : lower + length] == centre).astype(jnp.float32)[:, None]
        total = total + kernel[offset] * grid[lower : lower + length] * same
    return total


def norm_forward(mixed, norm_gain):
    centred = mixed - jnp.mean(mixed, -1, keepdims=True)
    variance = jnp.mean(centred * centred, -1, keepdims=True)
    scale_inv = lax.rsqrt(variance + EPS)
    normed = centred * scale_inv
    gated = normed * norm_gain
    sigma = jax.nn.sigmoid(gated)
    act = (gated * sigma).astype(jnp.bfloat16)
    return (normed, scale_inv, gated, sigma, act)


def norm_backward(grad_act, normed, scale_inv, gated, sigma, norm_gain):
    grad_gated = grad_act * sigma * (1.0 + gated * (1.0 - sigma))
    grad_normed = grad_gated * norm_gain
    grad_mixed = scale_inv * (
        grad_normed
        - jnp.mean(grad_normed, -1, keepdims=True)
        - normed * jnp.mean(grad_normed * normed, -1, keepdims=True)
    )
    return (grad_gated, grad_mixed)


def body(hidden, segment_ids, kernel, norm_gain, projection, cotangent):
    frames_local = hidden[0]
    length = frames_local.shape[0]
    width = frames_local.shape[1]
    taps = kernel.shape[0]
    reach = taps // 2
    start = lax.axis_index("seq") * length
    seg_row = jnp.pad(segment_ids[0], 2 * reach, constant_values=-1)
    seg_wide = lax.dynamic_slice_in_dim(seg_row, start, length + 4 * reach)
    seg_near = seg_wide[reach : reach + length + 2 * reach]
    grad_out = cotangent[0]
    received = padded_2(frames_local, (("seq", 0),), reach)
    mixed = depth_forward(received, seg_near, kernel, length)
    normed, scale_inv, gated, sigma, act = norm_forward(mixed, norm_gain)
    conv_out = jnp.dot(act, projection.T, preferred_element_type=jnp.float32).astype(jnp.bfloat16)
    grad_act = jnp.dot(grad_out, projection, preferred_element_type=jnp.float32)
    grad_gated, grad_mixed = norm_backward(grad_act, normed, scale_inv, gated, sigma, norm_gain)
    zeroed = jnp.pad(grad_mixed, ((2 * reach, 2 * reach), (0, 0)))
    partial_back = spread_back(zeroed, seg_wide, kernel, length + 2 * reach)
    from_lower = from_behind(partial_back[length + reach :].astype(jnp.bfloat16), "seq", 1).astype(
        jnp.float32
    )
    from_upper = from_behind(partial_back[:reach].astype(jnp.bfloat16), "seq", -1).astype(
        jnp.float32
    )
    inner = partial_back[reach : reach + length]
    grad_frames = inner.at[:reach].add(from_lower).at[length - reach :].add(from_upper)
    kernel_grad = kernel_terms(grad_mixed, received, seg_near, length, taps)
    gain_grad = jnp.sum(grad_gated * normed, 0)
    grad_hidden = grad_frames.astype(jnp.bfloat16)
    small_grads = jnp.concatenate([kernel_grad.T, gain_grad[:, None]], 1)
    weight_part = jnp.dot(grad_out.T, act, preferred_element_type=jnp.float32)
    shares = lax.psum_scatter(
        jnp.concatenate([weight_part, small_grads], 1), "seq", scatter_dimension=0, tiled=True
    )
    totals = lax.psum(shares, "dp")
    factor = 1.0 / math.sqrt(length * lax.axis_size("seq") * lax.axis_size("dp"))
    totals = totals * factor
    return (
        conv_out[None],
        grad_hidden[None],
        totals[:, :width],
        totals[:, width : width + taps],
        totals[:, width + taps],
    )


def solution(mesh):
    in_specs = (P("dp", "seq", None), P("dp", None), P(), P(), P(), P("dp", "seq", None))
    out_specs = (
        P("dp", "seq", None),
        P("dp", "seq", None),
        P("seq", None),
        P("seq", None),
        P("seq"),
    )
    return jax.shard_map(body, mesh=mesh, in_specs=in_specs, out_specs=out_specs, check_vma=False)
```

profile of v0, /device:TPU:0, one launch (start us, length us, event | category | flops | bytes accessed | tf_op | source)
XLA Modules:
  0.0 173.9 jit_solution(10372962789280943236)
XLA Ops:
  7.2 0.9 slice_bitcast_fusion.1
  8.2 2.4 %collective-permute-start = (bf16[15,1024]{1,0:T(8,128)(2,1)S(1)}, bf16[15,1024]{1,0:T(8,128)(2,1)S(1)}, u32[]{:S(2)}, u32[]{:S(2)}) collective-permute-start(bf16[15,1024]{1,0:T(8,128)(2,1)S(1)} %get-tuple-element.77), channel_id=1, source_target_pairs={{0,1},{1,2},{2,3},{3,4},{4,5},{5,6},{6,7},{8,9},{9,10},{10,11},{11... | collective-permute-start | bytes 92168 | tf_op jit(solution)/shard_map/ppermute | solution.py:18
  10.5 1.3 collective-permute-start.1
  11.8 0.8 pad_dynamic-slice_fusion
  12.8 1.1 fusion.280
  14.0 1.3 fusion.279
  15.4 0.3 collective-permute-done.1
  15.7 21.9 %fusion.276 = (f32[256]{0:T(256)S(1)}, f32[256,1024]{1,0:T(8,128)S(1)}) fusion(f32[256]{0:T(256)S(1)} %get-tuple-element.141, bf16[15,1024]{1,0:T(8,128)(2,1)S(1)} %collective-permute-done.1, bf16[256,1024]{1,0:T(8,128)(2,1)} %bitcast.88, f32[1024]{0:T(1024)S(1)} %bitcast.115, f32[256]{0:T(256)S(1)} %get-tuple-element.142, f32[1024]{0:T(1024)S(1)} %bitcast.117, ...), kind=kLoop, calls=%fused_computation.481 | loop fusion | flops 55836416 | bytes 1793024 | tf_op jit(solution)/shard_map/reduce_sum | solution.py:64
  37.6 0.2 multiply_reduce_fusion.2
  37.9 3.0 %convolution_bitcast_fusion = f32[1024,1024]{0,1:T(8,128)} fusion(bf16[1,256,1024]{2,1,0:T(8,128)(2,1)S(1)} %copy-done.6, f32[256,1024]{1,0:T(8,128)S(1)} %get-tuple-element.74, f32[1024]{0:T(1024)S(1)} %copy-done.5, f32[256]{0:T(256)S(1)} %add_rsqrt_fusion, f32[256]{0:T(256)S(1)} %broadcast_multiply_fusion.3), kind=kOutput, calls=%fused_computation.59 | convolution fusion | flops 538968064 | bytes 5773312 | tf_op jit(solution)/shard_map/dot_general | solution.py:116
  40.9 1.3 multiply_reduce_fusion
  42.2 2.8 %fusion.213 = (f32[1024]{0:T(1024)S(1)}, f32[1024]{0:T(1024)S(1)}, f32[1024]{0:T(1024)S(1)}, f32[1024]{0:T(1024)S(1)}, f32[1024]{0:T(1024)S(1)}, /*index=5*/f32[1024]{0:T(1024)S(1)}, f32[256,1024]{1,0:T(8,128)S(1)}) fusion(bf16[15,1024]{1,0:T(8,128)(2,1)S(1)} %collective-permute-done.1, bf16[256,1024]{1,0:T(8,128)(2,1)S(1)} %bitcast.89, ...), kind=kLoop, calls=%fused_computation.337 | loop fusion | flops 12838912 | bytes 3739648 | tf_op jit(solution)/shard_map/reduce_sum | solution.py:47
  45.2 1.5 fusion.161
  46.7 3.4 %fusion.189 = (f32[1024]{0:T(1024)S(1)}, f32[1024]{0:T(1024)S(1)}, f32[1024]{0:T(1024)S(1)}, f32[1024]{0:T(1024)S(1)}, f32[1024]{0:T(1024)S(1)}, /*index=5*/f32[1024]{0:T(1024)S(1)}) fusion(f32[256,1024]{1,0:T(8,128)S(1)} %get-tuple-element.70, f32[256]{0:T(256)S(1)} %get-tuple-element.147, bf16[15,1024]{1,0:T(8,128)(2,1)S(1)} %collective-permute-done.1, ...), kind=kLoop, calls=%fused_computation.313 | loop fusion | flops 11003904 | bytes 1634304 | tf_op jit(solution)/shard_map/reduce_sum | solution.py:47
  50.1 2.0 %fusion.171 = (f32[1024]{0:T(1024)S(1)}, f32[1024]{0:T(1024)S(1)}, f32[1024]{0:T(1024)S(1)}, f32[1024]{0:T(1024)S(1)}, f32[1024]{0:T(1024)S(1)}, /*index=5*/f32[1024]{0:T(1024)S(1)}) fusion(f32[256,1024]{1,0:T(8,128)S(1)} %get-tuple-element.70, f32[256]{0:T(256)S(1)} %get-tuple-element.154, bf16[15,1024]{1,0:T(8,128)(2,1)S(1)} %collective-permute-done.1, ...), kind=kLoop, calls=%fused_computation.295 | loop fusion | flops 11003904 | bytes 1665024 | tf_op jit(solution)/shard_map/reduce_sum | solution.py:47
  52.2 1.7 fusion.143
  53.9 0.2 stack.127
  54.1 12.1 %concatenate.44 = f32[1024,1056]{0,1:T(8,128)} concatenate(f32[1024,1024]{0,1:T(8,128)} %convolution_bitcast_fusion, f32[1024,31]{0,1:T(8,128)S(1)} %bitcast.94, f32[1024,1]{0,1:T(1,128)S(1)} %bitcast.189), dimensions={1} | concatenate | bytes 8650752 | tf_op jit(solution)/shard_map/concatenate | solution.py:118
  66.7 7.0 %fusion.274 = (bf16[286,1024]{1,0:T(8,128)(2,1)S(1)}, f32[286,1024]{1,0:T(8,128)S(1)}) fusion(f32[286]{0:T(512)S(1)} %get-tuple-element.138, f32[1024]{0:T(1024)S(1)} %bitcast.116, f32[286]{0:T(512)S(1)} %get-tuple-element.139, f32[1024]{0:T(1024)S(1)} %bitcast.118, f32[286]{0:T(512)S(1)} %get-tuple-element.111, f32[1024]{0:T(1024)S(1)} %bitcast.122, ...), kind=kLoop, calls=%fused_computation.480 | loop fusion | flops 26943488 | bytes 2967056 | tf_op jit(solution)/shard_map/convert.1
  73.7 4.9 %collective-permute-start.2 = (bf16[15,1024]{1,0:T(8,128)(2,1)S(1)}, bf16[15,1024]{1,0:T(8,128)(2,1)S(1)}, u32[]{:S(2)}, u32[]{:S(2)}) collective-permute-start(bf16[15,1024]{1,0:T(8,128)(2,1)S(1)} %get-tuple-element.76), channel_id=1, source_target_pairs={{0,1},{1,2},{2,3},{3,4},{4,5},{5,6},{6,7},{8,9},{9,10},{10,11},{11... | collective-permute-start | bytes 92168 | tf_op jit(solution)/shard_map/ppermute | solution.py:27
  78.6 1.7 fusion.1
  80.3 1.3 collective-permute-start.3
  81.7 41.2 %reduce-scatter.2.cloned.1.call-done = f32[128,1056]{0,1:T(8,128)} async-done(((f32[1024,1056]{0,1:T(8,128)}), f32[128,1056]{0,1:T(8,128)}) %reduce-scatter.2.cloned.1.call-update) | async-done | bytes 540688 | tf_op jit(solution)/shard_map/reduce_scatter | solution.py:117
  123.0 0.9 slice_add_fusion.1
  123.9 0.6 scatter-add.6
  124.5 0.3 scatter-add.9
  124.8 0.9 convert_bitcast_fusion
  125.7 38.1 %all-reduce.4.cloned.1.call-done = f32[128,1056]{0,1:T(8,128)} async-done(((f32[128,1056]{0,1:T(8,128)}), f32[128,1056]{0,1:T(8,128)}) %all-reduce.4.cloned.1.call-update) | async-done | bytes 540688 | tf_op jit(solution)/shard_map/psum | solution.py:120
  163.8 1.1 broadcast_multiply_fusion
  164.9 0.5 slice_bitcast_fusion.2
  165.4 0.6 slice.918
  166.1 1.0 copy.11
  (37 shorter events, 1.1 us)
Async XLA Ops:
  7.2 33.7 %copy-start = (bf16[1024,1024]{1,0:T(8,128)(2,1)S(1)}, bf16[1024,1024]{1,0:T(8,128)(2,1)}, u32[]{:S(2)}) copy-start(bf16[1024,1024]{1,0:T(8,128)(2,1)} %param.14) | copy-start | bytes 6291460
  7.2 115.8 %reduce-scatter.2.cloned.1.call-start = ((), (), s32[]{:S(2)}) async-start(), calls=%async_computation.1 | async-start | bytes 4866048 | tf_op jit(solution)/shard_map/reduce_scatter | solution.py:117
  8.2 7.2 %collective-permute-start = (bf16[15,1024]{1,0:T(8,128)(2,1)S(1)}, bf16[15,1024]{1,0:T(8,128)(2,1)S(1)}, u32[]{:S(2)}, u32[]{:S(2)}) collective-permute-start(bf16[15,1024]{1,0:T(8,128)(2,1)S(1)} %get-tuple-element.77), channel_id=1, source_target_pairs={{0,1},{1,2},{2,3},{3,4},{4,5},{5,6},{6,7},{8,9},{9,10},{10,11},{11... | collective-permute-start | bytes 92168 | tf_op jit(solution)/shard_map/ppermute | solution.py:18
  10.5 5.2 %collective-permute-start.1 = (bf16[15,1024]{1,0:T(8,128)(2,1)S(1)}, bf16[15,1024]{1,0:T(8,128)(2,1)S(1)}, u32[]{:S(2)}, u32[]{:S(2)}) collective-permute-start(bf16[15,1024]{1,0:T(8,128)(2,1)S(1)} %get-tuple-element.78), channel_id=1, source_target_pairs={{1,0},{2,1},{3,2},{4,3},{5,4},{6,5},{7,6},{9,8},{10,9},{11,10},{12... | collective-permute-start | bytes 92168 | tf_op jit(solution)/shard_map/ppermute | solution.py:19
  15.7 22.2 %copy-start.5 = (f32[1024]{0:T(1024)S(1)}, f32[1024]{0:T(1024)}, u32[]{:S(2)}) copy-start(f32[1024]{0:T(1024)} %param.13) | copy-start | bytes 12292
  15.7 22.2 %copy-start.6 = (bf16[1,256,1024]{2,1,0:T(8,128)(2,1)S(1)}, bf16[1,256,1024]{2,1,0:T(8,128)(2,1)}, u32[]{:S(2)}) copy-start(bf16[1,256,1024]{2,1,0:T(8,128)(2,1)} %param.15) | copy-start | bytes 1572868
  37.6 4.5 %copy-start.2 = (f32[256,1024]{1,0:T(8,128)}, f32[256,1024]{1,0:T(8,128)S(1)}, u32[]{:S(2)}) copy-start(f32[256,1024]{1,0:T(8,128)S(1)} %get-tuple-element.74) | copy-start | bytes 3145732
  40.9 1.3 copy-start.1
  66.3 97.5 %all-reduce.4.cloned.1.call-start = ((), (), s32[]{:S(2)}) async-start(), calls=%async_computation.2 | async-start | bytes 1081344 | tf_op jit(solution)/shard_map/psum | solution.py:120
  66.7 12.0 %copy-start.3 = (f32[256,1024]{1,0:T(8,128)S(1)}, f32[256,1024]{1,0:T(8,128)}, u32[]{:S(2)}) copy-start(f32[256,1024]{1,0:T(8,128)} %copy-done.2) | copy-start | bytes 3145732
  73.6 7.9 %copy-start.4 = (f32[286,1024]{1,0:T(8,128)}, f32[286,1024]{1,0:T(8,128)S(1)}, u32[]{:S(2)}) copy-start(f32[286,1024]{1,0:T(8,128)S(1)} %get-tuple-element.72) | copy-start | bytes 3514372
  73.7 49.3 %collective-permute-start.2 = (bf16[15,1024]{1,0:T(8,128)(2,1)S(1)}, bf16[15,1024]{1,0:T(8,128)(2,1)S(1)}, u32[]{:S(2)}, u32[]{:S(2)}) collective-permute-start(bf16[15,1024]{1,0:T(8,128)(2,1)S(1)} %get-tuple-element.76), channel_id=1, source_target_pairs={{0,1},{1,2},{2,3},{3,4},{4,5},{5,6},{6,7},{8,9},{9,10},{10,11},{11... | collective-permute-start | bytes 92168 | tf_op jit(solution)/shard_map/ppermute | solution.py:27
  80.3 44.2 %collective-permute-start.3 = (bf16[15,1024]{1,0:T(8,128)(2,1)S(1)}, bf16[15,1024]{1,0:T(8,128)(2,1)S(1)}, u32[]{:S(2)}, u32[]{:S(2)}) collective-permute-start(bf16[15,1024]{1,0:T(8,128)(2,1)S(1)} %get-tuple-element.75), channel_id=1, source_target_pairs={{1,0},{2,1},{3,2},{4,3},{5,4},{6,5},{7,6},{9,8},{10,9},{11,10},{12... | collective-permute-start | bytes 92168 | tf_op jit(solution)/shard_map/ppermute | solution.py:27
Sparse Core Ops, SparseCore 0:
  66.4 56.4 reduce-scatter.1
  125.3 38.4 all-reduce.3
where the time goes:
time: 175 us; the launch traced here: 174 us
  waiting for transfers between devices  79.7 us (46%)
  other arithmetic  44.3 us (25%)
  local copies, waits for them, and re-layouts  19.8 us (11%)
  between operations  14.3 us (8%)
  starting transfers between devices  9.95 us (6%)
  matrix products  5.87 us (3%)
    reduce_scatter x1, waiting for transfers between devices, body(): lax.psum_scatter(jnp.concatenate([weight_part, small_grads], 1), 'seq', s...  41.2 us
    psum x1, waiting for transfers between devices, body(): totals = lax.psum(shares, 'dp')  38.1 us
    reduce_sum x1, other arithmetic, norm_forward(): centred = mixed - jnp.mean(mixed, -1, keepdims=True)  21.9 us
    concatenate x1, local copies, waits for them, and re-layouts, body(): jnp.concatenate([weight_part, small_grads], 1)  12.1 us
    reduce_sum x6, other arithmetic, kernel_terms(): jnp.sum(grad * padded[offset:offset + length].astype(jnp.float32) * same, 0)  11.7 us
    another operation x1, other arithmetic  6.97 us
    ppermute x2, starting transfers between devices, from_behind(): lax.ppermute(value, axis, [(source, source + steps) for source in range(f...  6.22 us
  transfers between devices with their start and end apart: 6, of which 3 were waited for; matrix products, arithmetic and copies ran while one was open for 9% of the time, Pallas kernels for 0%

commit v1 on v0

v1 whole, which is shorter than its diff:
```python
import functools
import math

import jax
import jax.numpy as jnp
from jax import lax
from jax.experimental import pallas as pl
from jax.experimental.pallas import tpu as pltpu
from jax.sharding import PartitionSpec as P

EPS = 1e-05
LANES = 128
SUB = 8
CHUNK = 16
HALO = 32
EDGE = 16
MESH = pl.DeviceIdType.MESH
F32 = jnp.float32
BF16 = jnp.bfloat16


def row_mean(parts, width):
    total = parts[0]
    for part in parts[1:]:
        total = total + part
    return jnp.sum(total, axis=1, keepdims=True) * (1.0 / width)


def local_kernel(
    seg, hid, before, after, kern, gain, proj, cot,
    conv_out, grad_hidden, shares,
    mask, frames, cot_ext, cot_t, taps_b, grad_act, normed, sigma, inv, act, grad_mixed, gain_acc, small,
):
    length, width = hid.shape
    taps = kern.shape[0]
    reach = taps // 2
    slabs = width // LANES
    ext = length + 2 * EDGE
    cols = lambda s: pl.ds(s * LANES, LANES)

    for s in range(slabs):
        frames[s, :HALO, :] = before[:HALO, cols(s)].astype(F32)
        frames[s, HALO : HALO + length, :] = hid[:, cols(s)].astype(F32)
        frames[s, HALO + length :, :] = after[:HALO, cols(s)].astype(F32)
        for k in range(taps):
            taps_b[s, k] = jnp.broadcast_to(kern[k : k + 1, cols(s)], (SUB, LANES))
    cot_ext[:EDGE, :] = before[HALO:, :]
    cot_ext[EDGE : EDGE + length, :] = cot[...]
    cot_ext[EDGE + length :, :] = after[HALO:, :]
    cot_t[...] = cot[...].T
    gain_acc[...] = jnp.zeros_like(gain_acc)
    small[...] = jnp.zeros_like(small)

    @pl.loop(0, ext // SUB)
    def _(i):
        row = pl.multiple_of(i * SUB, SUB)
        own = seg[pl.ds(row + EDGE, SUB), :]
        for k in range(taps):
            there = seg[pl.ds(row + EDGE - reach + k, SUB), :]
            mask[k, pl.ds(row, SUB), :] = (there == own).astype(F32)

    @pl.loop(0, ext // CHUNK)
    def _(i):
        base = pl.multiple_of(i * CHUNK, CHUNK)
        tiles = CHUNK // SUB
        acc = [[jnp.zeros((SUB, LANES), F32) for _ in range(slabs)] for _ in range(tiles)]
        for k in range(taps):
            same = [mask[k, pl.ds(base + SUB * t, SUB), :] for t in range(tiles)]
            for s in range(slabs):
                tap = taps_b[s, k]
                for t in range(tiles):
                    there = frames[s, pl.ds(base + SUB * t + EDGE - reach + k, SUB), :]
                    acc[t][s] = acc[t][s] + tap * (there * same[t])
        acts = [[None] * slabs for _ in range(tiles)]
        for t in range(tiles):
            rows = pl.ds(base + SUB * t, SUB)
            mean = row_mean(acc[t], width)
            centred = [a - mean for a in acc[t]]
            var = row_mean([c * c for c in centred], width)
            scale = lax.rsqrt(var + EPS)
            inv[rows, :] = jnp.broadcast_to(scale, (SUB, LANES))
            for s in range(slabs):
                n = centred[s] * scale
                gated = n * gain[:, cols(s)]
                sig = jax.nn.sigmoid(gated)
                normed[rows, cols(s)] = n
                sigma[rows, cols(s)] = sig
                acts[t][s] = gated * sig
        for s in range(slabs):
            act[pl.ds(base, CHUNK), cols(s)] = jnp.concatenate([a[s] for a in acts], 0).astype(BF16)

    block = 256
    dims = lambda a, b: (((a,), (b,)), ((), ()))

    @pl.loop(0, width // block)
    def _(j):
        span = pl.ds(pl.multiple_of(j * block, block), block)
        shares[:, span] = lax.dot_general(
            cot_t[...], act[EDGE : EDGE + length, span], dims(1, 0), preferred_element_type=F32
        ).astype(BF16)
        grad_act[:, span] = lax.dot_general(
            cot_ext[...], proj[:, span], dims(1, 0), preferred_element_type=F32
        )
        conv_out[:, span] = lax.dot_general(
            act[EDGE : EDGE + length, :], proj[span, :], dims(1, 1), preferred_element_type=F32
        ).astype(BF16)

    @pl.loop(0, ext // SUB)
    def _(i):
        base = pl.multiple_of(i * SUB, SUB)
        rows = pl.ds(base, SUB)
        inside = jnp.logical_and(i >= EDGE // SUB, i < (EDGE + length) // SUB).astype(F32)
        ns, gns = [], []
        for s in range(slabs):
            n = normed[rows, cols(s)]
            sig = sigma[rows, cols(s)]
            g = gain[:, cols(s)]
            gg = grad_act[rows, cols(s)] * sig * (1.0 + n * g * (1.0 - sig))
            gain_acc[s] += inside * (gg * n)
            ns.append(n)
            gns.append(gg * g)
        m1 = row_mean(gns, width)
        m2 = row_mean([a * b for a, b in zip(gns, ns)], width)
        scale = inv[rows, :]
        for s in range(slabs):
            grad_mixed[s, rows, :] = scale * (gns[s] - m1 - ns[s] * m2)

    @pl.loop(0, slabs)
    def _(s):
        lanes = pl.ds(pl.multiple_of(s * LANES, LANES), LANES)

        def step(i, sums):
            base = pl.multiple_of(i * CHUNK, CHUNK)
            tiles = CHUNK // SUB
            sums = list(sums)
            outs = [jnp.zeros((SUB, LANES), F32) for _ in range(tiles)]
            here = [frames[s, pl.ds(base + HALO + SUB * t, SUB), :] for t in range(tiles)]
            for k in range(taps):
                back = taps - 1 - k
                tap = taps_b[s, k]
                for t in range(tiles):
                    row = base + EDGE + SUB * t
                    part = grad_mixed[s, pl.ds(row - reach + back, SUB), :] * mask[back, pl.ds(row, SUB), :]
                    outs[t] = outs[t] + tap * part
                    sums[k] = sums[k] + here[t] * part
            grad_hidden[pl.ds(base, CHUNK), lanes] = jnp.concatenate(outs, 0).astype(BF16)
            return tuple(sums)

        zeros = tuple(jnp.zeros((SUB, LANES), F32) for _ in range(taps))
        sums = lax.fori_loop(0, length // CHUNK, step, zeros)
        for k in range(taps):
            small[k : k + 1, :] = jnp.sum(sums[k], axis=0, keepdims=True)
        small[taps : taps + 1, :] = jnp.sum(gain_acc[s], axis=0, keepdims=True)
        shares[lanes, width:] = small[...].T.astype(BF16)


def local_part(seg, hid, before, after, kern, gain, proj, cot):
    length, width = hid.shape
    taps = kern.shape[0]
    slabs = width // LANES
    ext = length + 2 * EDGE
    vmem = pl.BlockSpec(memory_space=pltpu.VMEM)
    return pl.pallas_call(
        local_kernel,
        out_shape=(
            jax.ShapeDtypeStruct((length, width), BF16),
            jax.ShapeDtypeStruct((length, width), BF16),
            jax.ShapeDtypeStruct((width, width + LANES), BF16),
        ),
        in_specs=[vmem] * 8,
        out_specs=(vmem,) * 3,
        scratch_shapes=[
            pltpu.VMEM((taps, ext, LANES), F32),
            pltpu.VMEM((slabs, length + 2 * HALO, LANES), F32),
            pltpu.VMEM((ext, width), BF16),
            pltpu.VMEM((width, length), BF16),
            pltpu.VMEM((slabs, taps, SUB, LANES), F32),
            pltpu.VMEM((ext, width), F32),
            pltpu.VMEM((ext, width), F32),
            pltpu.VMEM((ext, width), F32),
            pltpu.VMEM((ext, LANES), F32),
            pltpu.VMEM((ext, width), BF16),
            pltpu.VMEM((slabs, ext, LANES), F32),
            pltpu.VMEM((slabs, SUB, LANES), F32),
            pltpu.VMEM((LANES, LANES), F32),
        ],
        compiler_params=pltpu.CompilerParams(vmem_limit_bytes=40 << 20),
        name="local_part",
    )(seg, hid, before, after, kern, gain, proj, cot)


def sum_kernel(
    n_dp, n_seq, factor,
    shares, out, tail,
    mate_in, chip_out, chip_in, total, dp_out, dp_in, gather,
    a_send, a_recv, b_send, b_recv, c_send, c_recv, d_send, d_recv,
):
    dp, seq = lax.axis_index("dp"), lax.axis_index("seq")
    chips = n_seq // 2
    chip, core = seq // 2, lax.rem(seq, 2)
    mate = chip * 2 + (1 - core)
    rows, width = total.shape
    wide = out.shape[1]
    split = dp_in.shape[1] != rows
    sub = dp_in.shape[1]

    barrier = pltpu.get_barrier_semaphore()
    pl.semaphore_signal(barrier, inc=1, device_id=(dp, mate), device_id_type=MESH)
    for d in range(1, chips):
        to = lax.rem(chip + d, chips) * 2 + core
        pl.semaphore_signal(barrier, inc=1, device_id=(dp, to), device_id_type=MESH)
    for d in range(1, n_dp):
        to = lax.rem(dp + d, n_dp)
        pl.semaphore_signal(barrier, inc=1, device_id=(to, seq), device_id_type=MESH)
    pl.semaphore_wait(barrier, 1 + (chips - 1) + (n_dp - 1))

    def block_of(c, k):
        return shares.at[pl.ds(pl.multiple_of((c * 2 + k) * rows, rows), rows), :]

    def to_mate(d):
        c = lax.rem(chip + d, chips)
        return pltpu.make_async_remote_copy(
            src_ref=block_of(c, 1 - core), dst_ref=mate_in.at[d],
            send_sem=a_send.at[d], recv_sem=a_recv.at[d],
            device_id=(dp, mate), device_id_type=MESH,
        )

    def to_chip(d):
        return pltpu.make_async_remote_copy(
            src_ref=chip_out.at[d], dst_ref=chip_in.at[d],
            send_sem=b_send.at[d], recv_sem=b_recv.at[d],
            device_id=(dp, lax.rem(chip + d, chips) * 2 + core), device_id_type=MESH,
        )

    order = list(range(1, chips)) + [0]
    for d in order:
        to_mate(d).start()
    for d in order:
        to_mate(d).wait_recv()
        c = lax.rem(chip + d, chips)
        pair = block_of(c, core)[...].astype(F32) + mate_in[d].astype(F32)
        if d:
            chip_out[d] = pair.astype(BF16)
            to_chip(d).start()
        else:
            total[...] = pair
    for d in range(1, chips):
        to_chip(d).wait_recv()
        total[...] += chip_in[d].astype(F32)

    def place(p):
        return pl.ds(pl.multiple_of(p * sub, sub), sub) if split else pl.ds(0, rows)

    dp_out[...] = total[...].astype(BF16)

    def to_group(d):
        to = lax.rem(dp + d, n_dp)
        return pltpu.make_async_remote_copy(
            src_ref=dp_out.at[place(to), :], dst_ref=dp_in.at[dp],
            send_sem=c_send.at[d], recv_sem=c_recv.at[d],
            device_id=(to, seq), device_id_type=MESH,
        )

    def from_group(d):
        at = lax.rem(dp - d + n_dp, n_dp)
        return pltpu.make_async_remote_copy(
            src_ref=dp_out.at[place(at), :], dst_ref=dp_in.at[at],
            send_sem=c_send.at[d], recv_sem=c_recv.at[d],
            device_id=(at, seq), device_id_type=MESH,
        )

    for d in range(1, n_dp):
        to_group(d).start()
    dp_in[dp] = dp_out[place(dp), :]
    for d in range(1, n_dp):
        from_group(d).wait_recv()
    done = dp_in[0].astype(F32)
    for p in range(1, n_dp):
        done = done + dp_in[p].astype(F32)
    done = done * factor
    if split:
        gather[place(dp), :] = done.astype(BF16)

        def to_all(d):
            return pltpu.make_async_remote_copy(
                src_ref=gather.at[place(dp), :], dst_ref=gather.at[place(dp), :],
                send_sem=d_send.at[d], recv_sem=d_recv.at[d],
                device_id=(lax.rem(dp + d, n_dp), seq), device_id_type=MESH,
            )

        def from_all(d):
            at = lax.rem(dp - d + n_dp, n_dp)
            return pltpu.make_async_remote_copy(
                src_ref=gather.at[place(at), :], dst_ref=gather.at[place(at), :],
                send_sem=d_send.at[d], recv_sem=d_recv.at[d],
                device_id=(at, seq), device_id_type=MESH,
            )

        for d in range(1, n_dp):
            to_all(d).start()
        for d in range(1, n_dp):
            from_all(d).wait_recv()
        out[...] = gather[:, :wide].astype(F32)
        tail[...] = gather[:, wide:].astype(F32)
        for d in range(1, n_dp):
            to_all(d).wait_send()
    else:
        out[...] = done[:, :wide]
        tail[...] = done[:, wide:]
    for d in order:
        to_mate(d).wait_send()
        if d:
            to_chip(d).wait_send()
    for d in range(1, n_dp):
        to_group(d).wait_send()


def sum_part(shares, n_dp, n_seq, factor):
    width = shares.shape[0]
    cols = shares.shape[1]
    rows = width // n_seq
    chips = n_seq // 2
    split = rows % (16 * n_dp) == 0
    sub = rows // n_dp if split else rows
    vmem = pl.BlockSpec(memory_space=pltpu.VMEM)
    sem = lambda n: pltpu.SemaphoreType.DMA((n,))
    return pl.pallas_call(
        functools.partial(sum_kernel, n_dp, n_seq, factor),
        out_shape=(
            jax.ShapeDtypeStruct((rows, width), F32),
            jax.ShapeDtypeStruct((rows, cols - width), F32),
        ),
        in_specs=[vmem],
        out_specs=(vmem, vmem),
        scratch_shapes=[
            pltpu.VMEM((chips, rows, cols), BF16),
            pltpu.VMEM((chips, rows, cols), BF16),
            pltpu.VMEM((chips, rows, cols), BF16),
            pltpu.VMEM((rows, cols), F32),
            pltpu.VMEM((rows, cols), BF16),
            pltpu.VMEM((n_dp, sub, cols), BF16),
            pltpu.VMEM((rows, cols), BF16),
            sem(chips), sem(chips), sem(chips), sem(chips),
            sem(n_dp), sem(n_dp), sem(n_dp), sem(n_dp),
        ],
        compiler_params=pltpu.CompilerParams(
            collective_id=0, has_side_effects=True, vmem_limit_bytes=24 << 20
        ),
        name="sum_part",
    )(shares)


def body(n_dp, n_seq, hidden, segment_ids, kernel, norm_gain, projection, cotangent):
    hid, cot = hidden[0], cotangent[0]
    length, width = hid.shape
    taps = kernel.shape[0]
    start = lax.axis_index("seq") * length
    seg_row = jnp.pad(segment_ids[0], HALO, constant_values=-1)
    seg_wide = lax.dynamic_slice_in_dim(seg_row, start, length + 2 * HALO)
    seg = jnp.broadcast_to(seg_wide[:, None], (length + 2 * HALO, LANES))
    up = [(i, i + 1) for i in range(n_seq - 1)]
    down = [(j, i) for i, j in up]
    before = lax.ppermute(jnp.concatenate([hid[length - HALO :], cot[length - EDGE :]], 0), "seq", up)
    after = lax.ppermute(jnp.concatenate([hid[:HALO], cot[:EDGE]], 0), "seq", down)
    gain = jnp.broadcast_to(norm_gain[None, :], (SUB, width))
    conv_out, grad_hidden, shares = local_part(seg, hid, before, after, kernel, gain, projection, cot)
    factor = 1.0 / math.sqrt(length * n_seq * n_dp)
    weight, tail = sum_part(shares, n_dp, n_seq, factor)
    return (conv_out[None], grad_hidden[None], weight, tail[:, :taps], tail[:, taps])


def solution(mesh):
    n_dp, n_seq = mesh.shape["dp"], mesh.shape["seq"]
    in_specs = (P("dp", "seq", None), P("dp", None), P(), P(), P(), P("dp", "seq", None))
    out_specs = (
        P("dp", "seq", None),
        P("dp", "seq", None),
        P("seq", None),
        P("seq", None),
        P("seq"),
    )
    return jax.shard_map(
        functools.partial(body, n_dp, n_seq), mesh=mesh, in_specs=in_specs, out_specs=out_specs, check_vma=False
    )
```

time: 175 us -> 84.6 us (0.48)
  waiting for transfers between devices: 79.7 us -> 3.21 us
  Pallas kernels: 0 us -> 66.5 us
  other arithmetic: 44.3 us -> 0.02 us
  between operations: 14.3 us -> 0.7 us
  local copies, waits for them, and re-layouts: 19.8 us -> 9.97 us
  starting transfers between devices: 9.95 us -> 3.65 us
  matrix products: 5.87 us -> 0 us
    pallas_call x0 -> x2, Pallas kernels: none -> 66.5 us  [the longest x1 36.7 us: sum_part(): pl.pallas_call(functools.partial(sum_kernel, n_dp, n_seq, factor), out_sh...]
    reduce_scatter x1 -> x0, waiting for transfers between devices: 41.2 us -> none  [body(): lax.psum_scatter(jnp.concatenate([weight_part, small_grads], 1), 'seq', s...]
    psum x1 -> x0, waiting for transfers between devices: 38.1 us -> none  [body(): totals = lax.psum(shares, 'dp')]
    reduce_sum x8 -> x0, other arithmetic: 33.8 us -> none  [the longest x1 21.9 us: norm_forward(): centred = mixed - jnp.mean(mixed, -1, keepdims=True)]
    concatenate x1 -> x0, local copies, waits for them, and re-layouts: 12.1 us -> none  [body(): jnp.concatenate([weight_part, small_grads], 1)]
    another operation x1 -> x0, other arithmetic: 6.97 us -> none
    ppermute x4 -> x2, starting transfers between devices: 9.87 us -> 3.65 us  [the longest x1 2.36 us: body(): lax.ppermute(jnp.concatenate([hid[length - HALO:], cot[length - EDGE:]],...]
    dot_general x3 -> x0, matrix products: 5.87 us -> none  [the longest x1 2.95 us: body(): weight_part = jnp.dot(grad_out.T, act, preferred_element_type=jnp.float32)]
  transfers between devices with their start and end apart: 6 -> 2, of which waited for: 3 -> 1; matrix products, arithmetic and copies ran while one was open for 9% -> 1% of each run, Pallas kernels for 0% -> 0%
where the time goes in v1:
time: 84.6 us; the launch traced here: 84.1 us
  Pallas kernels  66.5 us (79%)
  local copies, waits for them, and re-layouts  9.97 us (12%)
  starting transfers between devices  3.65 us (4%)
  waiting for transfers between devices  3.21 us (4%)
    pallas_call x1, Pallas kernels, sum_part(): pl.pallas_call(functools.partial(sum_kernel, n_dp, n_seq, factor), out_sh...  36.7 us
    pallas_call x1, Pallas kernels, local_part(): pl.pallas_call(local_kernel, out_shape=(jax.ShapeDtypeStruct((length, wid...  29.9 us
    unnamed x10, local copies, waits for them, and re-layouts  6.05 us
    ppermute x1, waiting for transfers between devices, body(): lax.ppermute(jnp.concatenate([hid[:HALO], cot[:EDGE]], 0), 'seq', down)  3.21 us
    ppermute x1, starting transfers between devices, body(): lax.ppermute(jnp.concatenate([hid[length - HALO:], cot[length - EDGE:]],...  2.36 us
  transfers between devices with their start and end apart: 2, of which 1 were waited for; matrix products, arithmetic and copies ran while one was open for 1% of the time, Pallas kernels for 0%

profile of v1, /device:TPU:0, one launch (start us, length us, event | category | flops | bytes accessed | tf_op | source)
XLA Modules:
  0.0 84.1 jit_solution(15890438372697813680)
XLA Ops:
  0.6 0.8 slice_bitcast_fusion.2
  1.4 0.9 %slice_bitcast_fusion = (bf16[32,1024]{1,0:T(8,128)(2,1)S(1)}, bf16[32,1024]{1,0:T(8,128)(2,1)S(1)}) fusion(bf16[1,256,1024]{2,1,0:T(8,128)(2,1)} %param.6), kind=kLoop, calls=%fused_computation.3 | loop fusion | bytes 262144 | tf_op jit(solution)/shard_map/slice | solution.py:364
  2.3 2.4 %collective-permute-start = (bf16[48,1024]{1,0:T(8,128)(2,1)S(1)}, bf16[48,1024]{1,0:T(8,128)(2,1)S(1)}, u32[]{:S(2)}, u32[]{:S(2)}) collective-permute-start(bf16[48,1024]{1,0:T(8,128)(2,1)S(1)} %pad_maximum_fusion), channel_id=1, source_target_pairs={{0,1},{1,2},{2,3},{3,4},{4,5},{5,6},{6,7},{8,9},{9,10},{10,11},{11... | collective-permute-start | bytes 294920 | tf_op jit(solution)/shard_map/ppermute | solution.py:363
  4.7 1.3 %collective-permute-start.1 = (bf16[48,1024]{1,0:T(8,128)(2,1)S(1)}, bf16[48,1024]{1,0:T(8,128)(2,1)S(1)}, u32[]{:S(2)}, u32[]{:S(2)}) collective-permute-start(bf16[48,1024]{1,0:T(8,128)(2,1)S(1)} %pad_maximum_fusion.1), channel_id=1, source_target_pairs={{1,0},{2,1},{3,2},{4,3},{5,4},{6,5},{7,6},{9,8},{10,9},{11,10},{12... | collective-permute-start | bytes 294920 | tf_op jit(solution)/shard_map/ppermute | solution.py:364
  6.0 0.8 pad_dynamic-slice_fusion
  6.8 0.0 collective-permute-done.before
  6.8 3.2 %collective-permute-done.1.after = bf16[48,1024]{1,0:T(8,128)(2,1)S(1)} collective-permute-done((bf16[48,1024]{1,0:T(8,128)(2,1)S(1)}, bf16[48,1024]{1,0:T(8,128)(2,1)S(1)}, u32[]{:S(2)}, u32[]{:S(2)}) %collective-permute-start.1) | collective-permute-done | bytes 98336 | tf_op jit(solution)/shard_map/ppermute | solution.py:364
  10.0 0.7 broadcast_in_dim.9.gain
  10.7 0.1 broadcast_in_dim.8.seg
  10.8 0.0 copy-start
  10.8 1.6 %copy-done = bf16[1024,1024]{1,0:T(8,128)(2,1)S(1)} copy-done((bf16[1024,1024]{1,0:T(8,128)(2,1)S(1)}, bf16[1024,1024]{1,0:T(8,128)(2,1)}, u32[]{:S(2)}) %copy-start) | copy-done | bytes 2097176
  12.4 0.0 copy-start.1
  12.4 1.0 %copy-done.1 = bf16[1,256,1024]{2,1,0:T(8,128)(2,1)S(1)} copy-done((bf16[1,256,1024]{2,1,0:T(8,128)(2,1)S(1)}, bf16[1,256,1024]{2,1,0:T(8,128)(2,1)}, u32[]{:S(2)}) %copy-start.1) | copy-done | bytes 524312
  13.4 0.0 copy-start.2
  13.4 1.0 %copy-done.2 = bf16[1,256,1024]{2,1,0:T(8,128)(2,1)S(1)} copy-done((bf16[1,256,1024]{2,1,0:T(8,128)(2,1)S(1)}, bf16[1,256,1024]{2,1,0:T(8,128)(2,1)}, u32[]{:S(2)}) %copy-start.2) | copy-done | bytes 524312
  14.5 0.0 copy-start.3
  14.5 0.9 %copy-done.3 = f32[31,1024]{1,0:T(8,128)S(1)} copy-done((f32[31,1024]{1,0:T(8,128)S(1)}, f32[31,1024]{1,0:T(8,128)}, u32[]{:S(2)}) %copy-start.3) | copy-done | bytes 127000
  15.4 29.9 %local_part.1 = (bf16[256,1024]{1,0:T(8,128)(2,1)}, bf16[256,1024]{1,0:T(8,128)(2,1)}, bf16[1024,1152]{1,0:T(8,128)(2,1)S(1)}) custom-call(s32[320,128]{1,0:T(8,128)S(1)} %broadcast_in_dim.8.seg, bf16[256,1024]{1,0:T(8,128)(2,1)S(1)} %bitcast.14, bf16[48,1024]{1,0:T(8,128)(2,1)S(1)} %collective-permute-done.before, ...), custom_call_target="tpu_custom_call" | custom-call | tf_op jit(solution)/shard_map/local_part/pallas_call | solution.py:163
  45.2 36.7 %sum_part.1 = (f32[128,1024]{1,0:T(8,128)S(1)}, f32[128,128]{1,0:T(8,128)S(1)}) custom-call(bf16[1024,1152]{1,0:T(8,128)(2,1)S(1)} %get-tuple-element.12.shares), custom_call_target="tpu_custom_call" | custom-call | tf_op jit(solution)/shard_map/sum_part/pallas_call | solution.py:327
  81.9 0.7 slice_reduce_fusion
  82.6 0.7 copy.12
  83.3 0.8 copy.14
  (2 shorter events, 0.0 us)
Async XLA Ops:
  2.3 4.5 %collective-permute-start = (bf16[48,1024]{1,0:T(8,128)(2,1)S(1)}, bf16[48,1024]{1,0:T(8,128)(2,1)S(1)}, u32[]{:S(2)}, u32[]{:S(2)}) collective-permute-start(bf16[48,1024]{1,0:T(8,128)(2,1)S(1)} %pad_maximum_fusion), channel_id=1, source_target_pairs={{0,1},{1,2},{2,3},{3,4},{4,5},{5,6},{6,7},{8,9},{9,10},{10,11},{11... | collective-permute-start | bytes 294920 | tf_op jit(solution)/shard_map/ppermute | solution.py:363
  4.7 5.3 %collective-permute-start.1 = (bf16[48,1024]{1,0:T(8,128)(2,1)S(1)}, bf16[48,1024]{1,0:T(8,128)(2,1)S(1)}, u32[]{:S(2)}, u32[]{:S(2)}) collective-permute-start(bf16[48,1024]{1,0:T(8,128)(2,1)S(1)} %pad_maximum_fusion.1), channel_id=1, source_target_pairs={{1,0},{2,1},{3,2},{4,3},{5,4},{6,5},{7,6},{9,8},{10,9},{11,10},{12... | collective-permute-start | bytes 294920 | tf_op jit(solution)/shard_map/ppermute | solution.py:364
  10.8 1.6 %copy-start = (bf16[1024,1024]{1,0:T(8,128)(2,1)S(1)}, bf16[1024,1024]{1,0:T(8,128)(2,1)}, u32[]{:S(2)}) copy-start(bf16[1024,1024]{1,0:T(8,128)(2,1)} %proj.1) | copy-start | bytes 6291460
  12.4 1.0 %copy-start.1 = (bf16[1,256,1024]{2,1,0:T(8,128)(2,1)S(1)}, bf16[1,256,1024]{2,1,0:T(8,128)(2,1)}, u32[]{:S(2)}) copy-start(bf16[1,256,1024]{2,1,0:T(8,128)(2,1)} %param.6) | copy-start | bytes 1572868
  13.4 1.0 %copy-start.2 = (bf16[1,256,1024]{2,1,0:T(8,128)(2,1)S(1)}, bf16[1,256,1024]{2,1,0:T(8,128)(2,1)}, u32[]{:S(2)}) copy-start(bf16[1,256,1024]{2,1,0:T(8,128)(2,1)} %param.11) | copy-start | bytes 1572868
  14.5 0.9 %copy-start.3 = (f32[31,1024]{1,0:T(8,128)S(1)}, f32[31,1024]{1,0:T(8,128)}, u32[]{:S(2)}) copy-start(f32[31,1024]{1,0:T(8,128)} %kern.1) | copy-start | bytes 380932

commit v2 on v1

v2 whole, which is shorter than its diff:
```python
import functools
import math

import jax
import jax.numpy as jnp
from jax import lax
from jax.experimental import pallas as pl
from jax.experimental.pallas import tpu as pltpu
from jax.sharding import PartitionSpec as P

EPS = 1e-05
LANES = 128
SUB = 8
CHUNK = 16
HALO = 32
EDGE = 16
MESH = pl.DeviceIdType.MESH
F32 = jnp.float32
BF16 = jnp.bfloat16


def row_mean(parts, width):
    total = parts[0]
    for part in parts[1:]:
        total = total + part
    return jnp.sum(total, axis=1, keepdims=True) * (1.0 / width)


def fused_kernel(
    n_dp, n_seq, factor,
    seg, kern, gain, hid, proj_in, cot,
    conv_out, grad_hidden, out, tail,
    mask, frames, hid_v, proj, edge_b, edge_a, cot_ext, cot_t, taps_b, grad_act, normed, sigma, inv, act,
    grad_mixed, gain_acc, small, turn, shares, mate_in, chip_out, chip_in, total, dp_out, dp_in, gather,
    small_in, small_sum, small_dp,
    l_sem, h_send, h_recv, a_send, a_recv, b_send, b_recv, c_send, c_recv, d_send, d_recv,
    e_send, e_recv, f_send, f_recv,
):
    length, width = hid.shape
    taps = kern.shape[0]
    reach = taps // 2
    slabs = width // LANES
    ext = length + 2 * EDGE
    inner = pl.ds(EDGE, length)
    cols = lambda s: pl.ds(s * LANES, LANES)
    dims = lambda a, b: (((a,), (b,)), ((), ()))

    dp, seq = lax.axis_index("dp"), lax.axis_index("seq")
    chips = n_seq // 2
    chip, core = seq // 2, lax.rem(seq, 2)
    mate = chip * 2 + (1 - core)
    right, left = lax.rem(seq + 1, n_seq), lax.rem(seq + n_seq - 1, n_seq)
    rows = out.shape[0]
    sub = dp_in.shape[1]
    split = sub != rows

    loads = [
        pltpu.make_async_copy(hid, hid_v, l_sem.at[0]),
        pltpu.make_async_copy(cot, cot_ext.at[inner, :], l_sem.at[1]),
        pltpu.make_async_copy(proj_in, proj, l_sem.at[2]),
    ]
    for load in loads:
        load.start()

    barrier = pltpu.get_barrier_semaphore()
    for d in range(1, n_seq):
        to = lax.rem(seq + d, n_seq)
        pl.semaphore_signal(barrier, inc=1, device_id=(dp, to), device_id_type=MESH)
    for d in range(1, n_dp):
        to = lax.rem(dp + d, n_dp)
        pl.semaphore_signal(barrier, inc=1, device_id=(to, seq), device_id_type=MESH)

    def remote(src, dst, send, recv, device):
        return pltpu.make_async_remote_copy(
            src_ref=src, dst_ref=dst, send_sem=send, recv_sem=recv, device_id=device, device_id_type=MESH
        )

    @pl.loop(0, ext // SUB)
    def _(i):
        row = pl.multiple_of(i * SUB, SUB)
        own = seg[pl.ds(row + EDGE, SUB), :]
        for k in range(taps):
            there = seg[pl.ds(row + EDGE - reach + k, SUB), :]
            mask[k, pl.ds(row, SUB), :] = (there == own).astype(F32)

    pl.semaphore_wait(barrier, (n_seq - 1) + (n_dp - 1))

    def edge_copies():
        return [
            remote(hid.at[pl.ds(length - HALO, HALO), :], edge_b, h_send.at[0], h_recv.at[0], (dp, right)),
            remote(hid.at[pl.ds(0, HALO), :], edge_a, h_send.at[1], h_recv.at[1], (dp, left)),
            remote(cot.at[pl.ds(length - EDGE, EDGE), :], cot_ext.at[pl.ds(0, EDGE), :],
                   h_send.at[2], h_recv.at[2], (dp, right)),
            remote(cot.at[pl.ds(0, EDGE), :], cot_ext.at[pl.ds(EDGE + length, EDGE), :],
                   h_send.at[3], h_recv.at[3], (dp, left)),
        ]

    edges = edge_copies()
    for copy in edges:
        copy.start()

    for s in range(slabs):
        for k in range(taps):
            taps_b[s, k] = jnp.broadcast_to(kern[k : k + 1, cols(s)], (SUB, LANES))
    gain_acc[...] = jnp.zeros_like(gain_acc)
    turn[...] = jnp.zeros_like(turn)
    loads[0].wait()
    for s in range(slabs):
        frames[s, HALO : HALO + length, :] = hid_v[:, cols(s)].astype(F32)
    loads[1].wait()
    cot_t[...] = cot_ext[inner, :].T

    def forward(i):
        base = pl.multiple_of(i * CHUNK, CHUNK)
        tiles = CHUNK // SUB
        acc = [[jnp.zeros((SUB, LANES), F32) for _ in range(slabs)] for _ in range(tiles)]
        for k in range(taps):
            same = [mask[k, pl.ds(base + SUB * t, SUB), :] for t in range(tiles)]
            for s in range(slabs):
                tap = taps_b[s, k]
                for t in range(tiles):
                    there = frames[s, pl.ds(base + SUB * t + EDGE - reach + k, SUB), :]
                    acc[t][s] = acc[t][s] + tap * (there * same[t])
        acts = [[None] * slabs for _ in range(tiles)]
        for t in range(tiles):
            at = pl.ds(base + SUB * t, SUB)
            mean = row_mean(acc[t], width)
            centred = [a - mean for a in acc[t]]
            var = row_mean([c * c for c in centred], width)
            scale = lax.rsqrt(var + EPS)
            inv[at, :] = jnp.broadcast_to(scale, (SUB, LANES))
            for s in range(slabs):
                n = centred[s] * scale
                gated = n * gain[:, cols(s)]
                sig = jax.nn.sigmoid(gated)
                normed[at, cols(s)] = n
                sigma[at, cols(s)] = sig
                acts[t][s] = gated * sig
        for s in range(slabs):
            act[pl.ds(base, CHUNK), cols(s)] = jnp.concatenate([a[s] for a in acts], 0).astype(BF16)

    count = ext // CHUNK

    @pl.loop(2, count - 2)
    def _(i):
        forward(i)

    edges[0].wait_recv()
    edges[1].wait_recv()
    for s in range(slabs):
        frames[s, :HALO, :] = edge_b[:, cols(s)].astype(F32)
        frames[s, HALO + length :, :] = edge_a[:, cols(s)].astype(F32)

    @pl.loop(0, 4)
    def _(i):
        forward(i + (i // 2) * (count - 4))

    def block_dot(c, k):
        at = pl.ds(pl.multiple_of((c * 2 + k) * rows, rows), rows)
        return lax.dot_general(cot_t[at, :], act[inner, :], dims(1, 0), preferred_element_type=F32)

    def to_mate(d):
        return remote(shares.at[d], mate_in.at[d], a_send.at[d], a_recv.at[d], (dp, mate))

    def to_chip(d):
        to = lax.rem(chip + d, chips) * 2 + core
        return remote(chip_out.at[d], chip_in.at[d], b_send.at[d], b_recv.at[d], (dp, to))

    order = list(range(1, chips)) + [0]
    for d in order:
        shares[d] = block_dot(lax.rem(chip + d, chips), 1 - core).astype(BF16)
        to_mate(d).start()

    for d in order:
        pair = block_dot(lax.rem(chip + d, chips), core)
        to_mate(d).wait_recv()
        pair = pair + mate_in[d].astype(F32)
        if d:
            chip_out[d] = pair.astype(BF16)
            to_chip(d).start()
        else:
            total[...] = pair

    loads[2].wait()
    edges[2].wait_recv()
    edges[3].wait_recv()
    block = 256

    @pl.loop(0, width // block)
    def _(j):
        span = pl.ds(pl.multiple_of(j * block, block), block)
        grad_act[:, span] = lax.dot_general(
            cot_ext[...], proj[:, span], dims(1, 0), preferred_element_type=F32
        )
        conv_out[:, span] = lax.dot_general(
            act[inner, :], proj[span, :], dims(1, 1), preferred_element_type=F32
        ).astype(BF16)

    @pl.loop(0, ext // SUB)
    def _(i):
        at = pl.ds(pl.multiple_of(i * SUB, SUB), SUB)
        inside = jnp.logical_and(i >= EDGE // SUB, i < (EDGE + length) // SUB).astype(F32)
        ns, gns = [], []
        for s in range(slabs):
            n = normed[at, cols(s)]
            sig = sigma[at, cols(s)]
            g = gain[:, cols(s)]
            gg = grad_act[at, cols(s)] * sig * (1.0 + n * g * (1.0 - sig))
            gain_acc[s] += inside * (gg * n)
            ns.append(n)
            gns.append(gg * g)
        m1 = row_mean(gns, width)
        m2 = row_mean([a * b for a, b in zip(gns, ns)], width)
        scale = inv[at, :]
        for s in range(slabs):
            grad_mixed[s, at, :] = scale * (gns[s] - m1 - ns[s] * m2)

    def slab_grads(s):
        lanes = pl.ds(pl.multiple_of(s * LANES, LANES), LANES)

        def step(i, sums):
            base = pl.multiple_of(i * CHUNK, CHUNK)
            tiles = CHUNK // SUB
            sums = list(sums)
            outs = [jnp.zeros((SUB, LANES), F32) for _ in range(tiles)]
            here = [frames[s, pl.ds(base + HALO + SUB * t, SUB), :] for t in range(tiles)]
            for k in range(taps):
                back = taps - 1 - k
                tap = taps_b[s, k]
                for t in range(tiles):
                    row = base + EDGE + SUB * t
                    part = grad_mixed[s, pl.ds(row - reach + back, SUB), :] * mask[back, pl.ds(row, SUB), :]
                    outs[t] = outs[t] + tap * part
                    sums[k] = sums[k] + here[t] * part
            grad_hidden[pl.ds(base, CHUNK), lanes] = jnp.concatenate(outs, 0).astype(BF16)
            return tuple(sums)

        zeros = tuple(jnp.zeros((SUB, LANES), F32) for _ in range(taps))
        sums = lax.fori_loop(0, length // CHUNK, step, zeros)
        for k in range(taps):
            small[s, k : k + 1, :] = jnp.sum(sums[k], axis=0, keepdims=True)
        small[s, taps : taps + 1, :] = jnp.sum(gain_acc[s], axis=0, keepdims=True)

    half = slabs // 2

    @pl.loop(0, half)
    def _(s):
        slab_grads(s)

    def place(p):
        return pl.ds(pl.multiple_of(p * sub, sub), sub) if split else pl.ds(0, rows)

    def group_at(d):
        return lax.rem(dp + d, n_dp), lax.rem(dp - d + n_dp, n_dp)

    def group_copy(d, slot, to):
        return remote(dp_out.at[place(to), :], dp_in.at[slot], c_send.at[d], c_recv.at[d], (to, seq))

    for d in range(1, chips):
        to_chip(d).wait_recv()
        total[...] += chip_in[d].astype(F32)
    dp_out[...] = total[...].astype(BF16)
    for d in range(1, n_dp):
        group_copy(d, dp, group_at(d)[0]).start()
    dp_in[dp] = dp_out[place(dp), :]

    @pl.loop(half, slabs)
    def _(s):
        slab_grads(s)

    def my_slab(j):
        return (j * rows) // LANES

    def small_copy(d, to):
        return remote(small.at[my_slab(to)], small_in.at[d], e_send.at[d], e_recv.at[d], (dp, to))

    for d in range(1, n_seq):
        small_copy(d, lax.rem(seq + d, n_seq)).start()

    for d in range(1, n_dp):
        group_copy(d, group_at(d)[1], group_at(d)[1]).wait_recv()
    done = dp_in[0].astype(F32)
    for p in range(1, n_dp):
        done = done + dp_in[p].astype(F32)
    done = done * factor

    def gather_copy(d, p, to):
        return remote(gather.at[place(p), :], gather.at[place(p), :], d_send.at[d], d_recv.at[d], (to, seq))

    if split:
        gather[place(dp), :] = done.astype(BF16)
        for d in range(1, n_dp):
            gather_copy(d, dp, group_at(d)[0]).start()
    else:
        out[...] = done

    mine = small[my_slab(seq)]
    for d in range(1, n_seq):
        small_copy(d, lax.rem(seq + d, n_seq)).wait_recv()
        mine = mine + small_in[d]
    small_sum[...] = mine

    def tail_copy(d, slot, to):
        return remote(small_sum, small_dp.at[slot], f_send.at[d], f_recv.at[d], (to, seq))

    for d in range(1, n_dp):
        tail_copy(d, dp, group_at(d)[0]).start()
    small_dp[dp] = mine

    if split:
        for d in range(1, n_dp):
            gather_copy(d, group_at(d)[1], group_at(d)[1]).wait_recv()
        out[...] = gather[...].astype(F32)

    for d in range(1, n_dp):
        tail_copy(d, group_at(d)[1], group_at(d)[1]).wait_recv()
    whole = small_dp[0]
    for p in range(1, n_dp):
        whole = whole + small_dp[p]
    turn[: taps + 1, :] = whole * factor
    turn[...] = turn[...].T
    tail[...] = turn[pl.ds(pl.multiple_of(lax.rem(seq * rows, LANES), min(rows, LANES)), rows), :]

    for copy in edges:
        copy.wait_send()
    for d in order:
        to_mate(d).wait_send()
        if d:
            to_chip(d).wait_send()
    for d in range(1, n_seq):
        small_copy(d, lax.rem(seq + d, n_seq)).wait_send()
    for d in range(1, n_dp):
        group_copy(d, dp, group_at(d)[0]).wait_send()
        tail_copy(d, dp, group_at(d)[0]).wait_send()
        if split:
            gather_copy(d, dp, group_at(d)[0]).wait_send()


def fused(seg, kern, gain, hid, proj, cot, n_dp, n_seq, factor):
    length, width = hid.shape
    taps = kern.shape[0]
    slabs = width // LANES
    ext = length + 2 * EDGE
    rows = width // n_seq
    chips = n_seq // 2
    split = rows % (16 * n_dp) == 0
    sub = rows // n_dp if split else rows
    vmem = pl.BlockSpec(memory_space=pltpu.VMEM)
    hbm = pl.BlockSpec(memory_space=pl.ANY)
    sem = lambda n: pltpu.SemaphoreType.DMA((n,))
    return pl.pallas_call(
        functools.partial(fused_kernel, n_dp, n_seq, factor),
        out_shape=(
            jax.ShapeDtypeStruct((length, width), BF16),
            jax.ShapeDtypeStruct((length, width), BF16),
            jax.ShapeDtypeStruct((rows, width), F32),
            jax.ShapeDtypeStruct((rows, LANES), F32),
        ),
        in_specs=[vmem] * 3 + [hbm] * 3,
        out_specs=(vmem,) * 4,
        scratch_shapes=[
            pltpu.VMEM((taps, ext, LANES), F32),
            pltpu.VMEM((slabs, length + 2 * HALO, LANES), F32),
            pltpu.VMEM((length, width), BF16),
            pltpu.VMEM((width, width), BF16),
            pltpu.VMEM((HALO, width), BF16),
            pltpu.VMEM((HALO, width), BF16),
            pltpu.VMEM((ext, width), BF16),
            pltpu.VMEM((width, length), BF16),
            pltpu.VMEM((slabs, taps, SUB, LANES), F32),
            pltpu.VMEM((ext, width), F32),
            pltpu.VMEM((ext, width), F32),
            pltpu.VMEM((ext, width), F32),
            pltpu.VMEM((ext, LANES), F32),
            pltpu.VMEM((ext, width), BF16),
            pltpu.VMEM((slabs, ext, LANES), F32),
            pltpu.VMEM((slabs, SUB, LANES), F32),
            pltpu.VMEM((slabs, taps + 1, LANES), F32),
            pltpu.VMEM((LANES, LANES), F32),
            pltpu.VMEM((chips, rows, width), BF16),
            pltpu.VMEM((chips, rows, width), BF16),
            pltpu.VMEM((chips, rows, width), BF16),
            pltpu.VMEM((chips, rows, width), BF16),
            pltpu.VMEM((rows, width), F32),
            pltpu.VMEM((rows, width), BF16),
            pltpu.VMEM((n_dp, sub, width), BF16),
            pltpu.VMEM((rows, width), BF16),
            pltpu.VMEM((n_seq, taps + 1, LANES), F32),
            pltpu.VMEM((taps + 1, LANES), F32),
            pltpu.VMEM((n_dp, taps + 1, LANES), F32),
            sem(3), sem(4), sem(4), sem(chips), sem(chips), sem(chips), sem(chips),
            sem(n_dp), sem(n_dp), sem(n_dp), sem(n_dp), sem(n_seq), sem(n_seq), sem(n_dp), sem(n_dp),
        ],
        compiler_params=pltpu.CompilerParams(
            collective_id=0, has_side_effects=True, vmem_limit_bytes=48 << 20
        ),
        name="fused",
    )(seg, kern, gain, hid, proj, cot)


def body(n_dp, n_seq, hidden, segment_ids, kernel, norm_gain, projection, cotangent):
    hid, cot = hidden[0], cotangent[0]
    length, width = hid.shape
    taps = kernel.shape[0]
    start = lax.axis_index("seq") * length
    seg_row = jnp.pad(segment_ids[0], HALO, constant_values=-1)
    seg_wide = lax.dynamic_slice_in_dim(seg_row, start, length + 2 * HALO)
    seg = jnp.broadcast_to(seg_wide[:, None], (length + 2 * HALO, LANES))
    gain = norm_gain[None, :]
    factor = 1.0 / math.sqrt(length * n_seq * n_dp)
    conv_out, grad_hidden, weight, tail = fused(
        seg, kernel, gain, hid, projection, cot, n_dp, n_seq, factor
    )
    return (conv_out[None], grad_hidden[None], weight, tail[:, :taps], tail[:, taps])


def solution(mesh):
    n_dp, n_seq = mesh.shape["dp"], mesh.shape["seq"]
    in_specs = (P("dp", "seq", None), P("dp", None), P(), P(), P(), P("dp", "seq", None))
    out_specs = (
        P("dp", "seq", None),
        P("dp", "seq", None),
        P("seq", None),
        P("seq", None),
        P("seq"),
    )
    return jax.shard_map(
        functools.partial(body, n_dp, n_seq), mesh=mesh, in_specs=in_specs, out_specs=out_specs, check_vma=False
    )
```

time: 84.6 us -> 57.8 us (0.68)
  Pallas kernels: 66.5 us -> 46.9 us
  starting transfers between devices: 3.65 us -> 0 us
  waiting for transfers between devices: 3.21 us -> 0 us
    pallas_call x2 -> x1, Pallas kernels: 66.5 us -> 46.9 us  [fused(): pl.pallas_call(functools.partial(fused_kernel, n_dp, n_seq, factor), out_...]
    ppermute x2 -> x0, starting transfers between devices: 3.65 us -> none  [the longest x1 2.36 us: body(): lax.ppermute(jnp.concatenate([hid[length - HALO:], cot[length - EDGE:]],...]
    ppermute x2 -> x0, waiting for transfers between devices: 3.21 us -> none  [the longest x1 3.21 us: body(): lax.ppermute(jnp.concatenate([hid[:HALO], cot[:EDGE]], 0), 'seq', down)]
    unnamed x10 -> x14, local copies, waits for them, and re-layouts: 6.05 us -> 8.33 us
    slice x2 -> x0, local copies, waits for them, and re-layouts: 1.66 us -> none  [the longest x1 0.88 us: body(): hid[:HALO]]
  transfers between devices with their start and end apart: 2 -> 0, of which waited for: 1 -> 0; matrix products, arithmetic and copies ran while one was open for 1% -> 0% of each run, Pallas kernels for 0% -> 0%
where the time goes in v2:
time: 57.8 us; the launch traced here: 57.5 us
  Pallas kernels  46.9 us (81%)
  local copies, waits for them, and re-layouts  9.9 us (17%)
  between operations  0.67 us (1%)
    pallas_call x1, Pallas kernels, fused(): pl.pallas_call(functools.partial(fused_kernel, n_dp, n_seq, factor), out_...  46.9 us
    unnamed x14, local copies, waits for them, and re-layouts  8.33 us

profile of v2, /device:TPU:0, one launch (start us, length us, event | category | flops | bytes accessed | tf_op | source)
XLA Modules:
  0.0 57.5 jit_solution(8841389371275147234)
XLA Ops:
  0.6 0.8 %pad_dynamic-slice_fusion = s32[320]{0:T(512)S(1)} fusion(s32[]{:T(128)S(6)} %select_n.3, s32[2048]{0:T(1024)} %bitcast.13), kind=kLoop, calls=%fused_computation.1 | loop fusion | bytes 9476 | tf_op jit(solution)/shard_map/dynamic_slice | solution.py:407
  1.4 0.1 broadcast_in_dim.15.seg
  1.5 0.0 copy-start
  1.5 1.6 %copy-done = bf16[1024,1024]{1,0:T(8,128)(2,1)S(1)} copy-done((bf16[1024,1024]{1,0:T(8,128)(2,1)S(1)}, bf16[1024,1024]{1,0:T(8,128)(2,1)}, u32[]{:S(2)}) %copy-start) | copy-done | bytes 2097176
  3.1 0.0 copy-start.1
  3.1 1.0 %copy-done.1 = bf16[1,256,1024]{2,1,0:T(8,128)(2,1)S(1)} copy-done((bf16[1,256,1024]{2,1,0:T(8,128)(2,1)S(1)}, bf16[1,256,1024]{2,1,0:T(8,128)(2,1)}, u32[]{:S(2)}) %copy-start.1) | copy-done | bytes 524312
  4.2 0.0 copy-start.2
  4.2 1.0 %copy-done.2 = bf16[1,256,1024]{2,1,0:T(8,128)(2,1)S(1)} copy-done((bf16[1,256,1024]{2,1,0:T(8,128)(2,1)S(1)}, bf16[1,256,1024]{2,1,0:T(8,128)(2,1)}, u32[]{:S(2)}) %copy-start.2) | copy-done | bytes 524312
  5.2 0.0 copy-start.3
  5.2 0.9 %copy-done.3 = f32[31,1024]{1,0:T(8,128)S(1)} copy-done((f32[31,1024]{1,0:T(8,128)S(1)}, f32[31,1024]{1,0:T(8,128)}, u32[]{:S(2)}) %copy-start.3) | copy-done | bytes 127000
  6.1 0.0 copy-start.4
  6.1 0.7 %copy-done.4 = f32[1024]{0:T(1024)S(1)} copy-done((f32[1024]{0:T(1024)S(1)}, f32[1024]{0:T(1024)}, u32[]{:S(2)}) %copy-start.4) | copy-done | bytes 4120
  6.8 46.9 %fused.1 = (bf16[256,1024]{1,0:T(8,128)(2,1)S(1)}, bf16[256,1024]{1,0:T(8,128)(2,1)S(1)}, f32[128,1024]{1,0:T(8,128)S(1)}, f32[128,128]{1,0:T(8,128)S(1)}) custom-call(s32[320,128]{1,0:T(8,128)S(1)} %broadcast_in_dim.15.seg, f32[31,1024]{1,0:T(8,128)S(1)} %copy-done.3, f32[1,1024]{1,0:T(1,128)S(1)} %bitcast.12, bf16[256,1024]{1,0:T(8,128)(2,1)S(1)} %bitcast.9, ...), custom_call_target="tpu_custom_call" | custom-call | tf_op jit(solution)/shard_map/fused/pallas_call | solution.py:351
  53.7 0.7 %copy.12 = f32[128,31]{0,1:T(8,128)} copy(f32[128,31]{1,0:T(8,128)S(1)} %bitcast.11) | data formatting | bytes 31744
  54.4 0.7 %slice_reduce_fusion = f32[128]{0:T(128)} fusion(f32[128,128]{1,0:T(8,128)S(1)} %get-tuple-element.12), kind=kLoop, calls=%fused_computation | loop fusion | bytes 1024 | tf_op jit(solution)/shard_map/slice | solution.py:414
  55.1 0.8 %copy.16 = bf16[1,256,1024]{2,1,0:T(8,128)(2,1)} copy(bf16[1,256,1024]{2,1,0:T(8,128)(2,1)S(1)} %bitcast.8) | data formatting | bytes 1048576
  55.9 0.8 %copy.17 = bf16[1,256,1024]{2,1,0:T(8,128)(2,1)} copy(bf16[1,256,1024]{2,1,0:T(8,128)(2,1)S(1)} %bitcast.7) | data formatting | bytes 1048576
  56.7 0.8 %copy.18 = f32[128,1024]{1,0:T(8,128)} copy(f32[128,1024]{1,0:T(8,128)S(1)} %get-tuple-element.30) | data formatting | bytes 1048576
Async XLA Ops:
  1.5 1.6 %copy-start = (bf16[1024,1024]{1,0:T(8,128)(2,1)S(1)}, bf16[1024,1024]{1,0:T(8,128)(2,1)}, u32[]{:S(2)}) copy-start(bf16[1024,1024]{1,0:T(8,128)(2,1)} %proj_in.1) | copy-start | bytes 6291460
  3.1 1.0 %copy-start.1 = (bf16[1,256,1024]{2,1,0:T(8,128)(2,1)S(1)}, bf16[1,256,1024]{2,1,0:T(8,128)(2,1)}, u32[]{:S(2)}) copy-start(bf16[1,256,1024]{2,1,0:T(8,128)(2,1)} %param.6) | copy-start | bytes 1572868
  4.2 1.0 %copy-start.2 = (bf16[1,256,1024]{2,1,0:T(8,128)(2,1)S(1)}, bf16[1,256,1024]{2,1,0:T(8,128)(2,1)}, u32[]{:S(2)}) copy-start(bf16[1,256,1024]{2,1,0:T(8,128)(2,1)} %param.11) | copy-start | bytes 1572868
  5.2 0.9 %copy-start.3 = (f32[31,1024]{1,0:T(8,128)S(1)}, f32[31,1024]{1,0:T(8,128)}, u32[]{:S(2)}) copy-start(f32[31,1024]{1,0:T(8,128)} %kern.1) | copy-start | bytes 380932
  6.1 0.7 %copy-start.4 = (f32[1024]{0:T(1024)S(1)}, f32[1024]{0:T(1024)}, u32[]{:S(2)}) copy-start(f32[1024]{0:T(1024)} %param.9) | copy-start | bytes 12292

commit v3 on v2

--- a/solution.py
+++ b/solution.py
@@ -28,8 +28,9 @@
 
 def fused_kernel(
     n_dp, n_seq, factor,
-    seg, kern, gain, hid, proj_in, cot,
-    conv_out, grad_hidden, out, tail,
+    seg, kern_in, gain_in, hid, proj_in, cot,
+    conv_to, hidden_to, out, tail,
+    kern, gain, conv_out, grad_hidden,
     mask, frames, hid_v, proj, edge_b, edge_a, cot_ext, cot_t, taps_b, grad_act, normed, sigma, inv, act,
     grad_mixed, gain_acc, small, turn, shares, mate_in, chip_out, chip_in, total, dp_out, dp_in, gather,
     small_in, small_sum, small_dp,
@@ -51,14 +52,21 @@
     mate = chip * 2 + (1 - core)
     right, left = lax.rem(seq + 1, n_seq), lax.rem(seq + n_seq - 1, n_seq)
     rows = out.shape[0]
-    sub = dp_in.shape[1]
+    sub = dp_in.shape[2]
+    parts = shares.shape[0]
+    part = width // parts
+    piece = lambda h: pl.ds(h * part, part)
     split = sub != rows
 
     loads = [
         pltpu.make_async_copy(hid, hid_v, l_sem.at[0]),
         pltpu.make_async_copy(cot, cot_ext.at[inner, :], l_sem.at[1]),
         pltpu.make_async_copy(proj_in, proj, l_sem.at[2]),
+        pltpu.make_async_copy(kern_in, kern, l_sem.at[3]),
+        pltpu.make_async_copy(gain_in, gain, l_sem.at[4]),
     ]
+    conv_store = pltpu.make_async_copy(conv_out, conv_to, l_sem.at[5])
+    hidden_store = pltpu.make_async_copy(grad_hidden, hidden_to, l_sem.at[6])
     for load in loads:
         load.start()
 
@@ -99,6 +107,8 @@
     for copy in edges:
         copy.start()
 
+    loads[3].wait()
+    loads[4].wait()
     for s in range(slabs):
         for k in range(taps):
             taps_b[s, k] = jnp.broadcast_to(kern[k : k + 1, cols(s)], (SUB, LANES))
@@ -151,35 +161,41 @@
         frames[s, :HALO, :] = edge_b[:, cols(s)].astype(F32)
         frames[s, HALO + length :, :] = edge_a[:, cols(s)].astype(F32)
 
-    @pl.loop(0, 4)
+    @pl.loop(0, 2)
     def _(i):
-        forward(i + (i // 2) * (count - 4))
-
-    def block_dot(c, k):
+        forward(1 + i * (count - 3))
+
+    def block_dot(h, c, k):
         at = pl.ds(pl.multiple_of((c * 2 + k) * rows, rows), rows)
-        return lax.dot_general(cot_t[at, :], act[inner, :], dims(1, 0), preferred_element_type=F32)
-
-    def to_mate(d):
-        return remote(shares.at[d], mate_in.at[d], a_send.at[d], a_recv.at[d], (dp, mate))
-
-    def to_chip(d):
+        return lax.dot_general(cot_t[at, :], act[inner, piece(h)], dims(1, 0), preferred_element_type=F32)
+
+    def to_mate(h, d):
+        return remote(shares.at[h, d], mate_in.at[h, d], a_send.at[h, d], a_recv.at[h, d], (dp, mate))
+
+    def to_chip(h, d):
         to = lax.rem(chip + d, chips) * 2 + core
-        return remote(chip_out.at[d], chip_in.at[d], b_send.at[d], b_recv.at[d], (dp, to))
+        return remote(chip_out.at[h, d], chip_in.at[h, d], b_send.at[h, d], b_recv.at[h, d], (dp, to))
 
     order = list(range(1, chips)) + [0]
-    for d in order:
-        shares[d] = block_dot(lax.rem(chip + d, chips), 1 - core).astype(BF16)
-        to_mate(d).start()
-
-    for d in order:
-        pair = block_dot(lax.rem(chip + d, chips), core)
-        to_mate(d).wait_recv()
-        pair = pair + mate_in[d].astype(F32)
-        if d:
-            chip_out[d] = pair.astype(BF16)
-            to_chip(d).start()
-        else:
-            total[...] = pair
+    for h in range(parts):
+        for d in order:
+            shares[h, d] = block_dot(h, lax.rem(chip + d, chips), 1 - core).astype(BF16)
+            to_mate(h, d).start()
+
+    for h in range(parts):
+        for d in order:
+            pair = block_dot(h, lax.rem(chip + d, chips), core)
+            to_mate(h, d).wait_recv()
+            pair = pair + mate_in[h, d].astype(F32)
+            if d:
+                chip_out[h, d] = pair.astype(BF16)
+                to_chip(h, d).start()
+            else:
+                total[:, piece(h)] = pair
+
+    @pl.loop(0, 2)
+    def _(i):
+        forward(i * (count - 1))
 
     loads[2].wait()
     edges[2].wait_recv()
@@ -195,6 +211,8 @@
         conv_out[:, span] = lax.dot_general(
             act[inner, :], proj[span, :], dims(1, 1), preferred_element_type=F32
         ).astype(BF16)
+
+    conv_store.start()
 
     @pl.loop(0, ext // SUB)
     def _(i):
@@ -241,32 +259,59 @@
             small[s, k : k + 1, :] = jnp.sum(sums[k], axis=0, keepdims=True)
         small[s, taps : taps + 1, :] = jnp.sum(gain_acc[s], axis=0, keepdims=True)
 
-    half = slabs // 2
-
-    @pl.loop(0, half)
-    def _(s):
-        slab_grads(s)
-
     def place(p):
         return pl.ds(pl.multiple_of(p * sub, sub), sub) if split else pl.ds(0, rows)
 
     def group_at(d):
         return lax.rem(dp + d, n_dp), lax.rem(dp - d + n_dp, n_dp)
 
-    def group_copy(d, slot, to):
-        return remote(dp_out.at[place(to), :], dp_in.at[slot], c_send.at[d], c_recv.at[d], (to, seq))
-
-    for d in range(1, chips):
-        to_chip(d).wait_recv()
-        total[...] += chip_in[d].astype(F32)
-    dp_out[...] = total[...].astype(BF16)
-    for d in range(1, n_dp):
-        group_copy(d, dp, group_at(d)[0]).start()
-    dp_in[dp] = dp_out[place(dp), :]
-
-    @pl.loop(half, slabs)
-    def _(s):
-        slab_grads(s)
+    def group_copy(h, d, slot, to):
+        return remote(
+            dp_out.at[h, place(to), :], dp_in.at[h, slot], c_send.at[h, d], c_recv.at[h, d], (to, seq)
+        )
+
+    def gather_copy(h, d, p, to):
+        return remote(
+            gather.at[h, place(p), :], gather.at[h, place(p), :], d_send.at[h, d], d_recv.at[h, d], (to, seq)
+        )
+
+    def sum_chips(h):
+        own = total[:, piece(h)]
+        for d in range(1, chips):
+            to_chip(h, d).wait_recv()
+            own = own + chip_in[h, d].astype(F32)
+        dp_out[h] = own.astype(BF16)
+        for d in range(1, n_dp):
+            group_copy(h, d, dp, group_at(d)[0]).start()
+        dp_in[h, dp] = dp_out[h, place(dp), :]
+
+    def sum_groups(h):
+        for d in range(1, n_dp):
+            group_copy(h, d, group_at(d)[1], group_at(d)[1]).wait_recv()
+        done = dp_in[h, 0].astype(F32)
+        for p in range(1, n_dp):
+            done = done + dp_in[h, p].astype(F32)
+        done = done * factor
+        if split:
+            gather[h, place(dp), :] = done.astype(BF16)
+            for d in range(1, n_dp):
+                gather_copy(h, d, dp, group_at(d)[0]).start()
+        else:
+            out[:, piece(h)] = done
+
+    def slabs_between(first, last):
+        @pl.loop(first, last)
+        def _(s):
+            slab_grads(s)
+
+    quarter = slabs // 4
+    sum_chips(0)
+    slabs_between(0, 2 * quarter)
+    sum_chips(1)
+    sum_groups(0)
+    slabs_between(2 * quarter, 3 * quarter)
+    sum_groups(1)
+    slabs_between(3 * quarter, slabs)
 
     def my_slab(j):
         return (j * rows) // LANES
@@ -276,23 +321,7 @@
 
     for d in range(1, n_seq):
         small_copy(d, lax.rem(seq + d, n_seq)).start()
-
-    for d in range(1, n_dp):
-        group_copy(d, group_at(d)[1], group_at(d)[1]).wait_recv()
-    done = dp_in[0].astype(F32)
-    for p in range(1, n_dp):
-        done = done + dp_in[p].astype(F32)
-    done = done * factor
-
-    def gather_copy(d, p, to):
-        return remote(gather.at[place(p), :], gather.at[place(p), :], d_send.at[d], d_recv.at[d], (to, seq))
-
-    if split:
-        gather[place(dp), :] = done.astype(BF16)
-        for d in range(1, n_dp):
-            gather_copy(d, dp, group_at(d)[0]).start()
-    else:
-        out[...] = done
+    hidden_store.start()
 
     mine = small[my_slab(seq)]
     for d in range(1, n_seq):
@@ -308,9 +337,10 @@
     small_dp[dp] = mine
 
     if split:
-        for d in range(1, n_dp):
-            gather_copy(d, group_at(d)[1], group_at(d)[1]).wait_recv()
-        out[...] = gather[...].astype(F32)
+        for h in range(parts):
+            for d in range(1, n_dp):
+                gather_copy(h, d, group_at(d)[1], group_at(d)[1]).wait_recv()
+            out[:, piece(h)] = gather[h].astype(F32)
 
     for d in range(1, n_dp):
         tail_copy(d, group_at(d)[1], group_at(d)[1]).wait_recv()
@@ -323,17 +353,21 @@
 
     for copy in edges:
         copy.wait_send()
-    for d in order:
-        to_mate(d).wait_send()
-        if d:
-            to_chip(d).wait_send()
+    for h in range(parts):
+        for d in order:
+            to_mate(h, d).wait_send()
+            if d:
+                to_chip(h, d).wait_send()
+        for d in range(1, n_dp):
+            group_copy(h, d, dp, group_at(d)[0]).wait_send()
+            if split:
+                gather_copy(h, d, dp, group_at(d)[0]).wait_send()
     for d in range(1, n_seq):
         small_copy(d, lax.rem(seq + d, n_seq)).wait_send()
     for d in range(1, n_dp):
-        group_copy(d, dp, group_at(d)[0]).wait_send()
         tail_copy(d, dp, group_at(d)[0]).wait_send()
-        if split:
-            gather_copy(d, dp, group_at(d)[0]).wait_send()
+    conv_store.wait()
+    hidden_store.wait()
 
 
 def fused(seg, kern, gain, hid, proj, cot, n_dp, n_seq, factor):
@@ -347,7 +381,9 @@
     sub = rows // n_dp if split else rows
     vmem = pl.BlockSpec(memory_space=pltpu.VMEM)
     hbm = pl.BlockSpec(memory_space=pl.ANY)
-    sem = lambda n: pltpu.SemaphoreType.DMA((n,))
+    parts = 2
+    part = width // parts
+    sem = lambda *n: pltpu.SemaphoreType.DMA(n)
     return pl.pallas_call(
         functools.partial(fused_kernel, n_dp, n_seq, factor),
         out_shape=(
@@ -356,9 +392,13 @@
             jax.ShapeDtypeStruct((rows, width), F32),
             jax.ShapeDtypeStruct((rows, LANES), F32),
         ),
-        in_specs=[vmem] * 3 + [hbm] * 3,
-        out_specs=(vmem,) * 4,
+        in_specs=[vmem] + [hbm] * 5,
+        out_specs=(hbm, hbm, vmem, vmem),
         scratch_shapes=[
+            pltpu.VMEM((taps, width), F32),
+            pltpu.VMEM((1, width), F32),
+            pltpu.VMEM((length, width), BF16),
+            pltpu.VMEM((length, width), BF16),
             pltpu.VMEM((taps, ext, LANES), F32),
             pltpu.VMEM((slabs, length + 2 * HALO, LANES), F32),
             pltpu.VMEM((length, width), BF16),
@@ -377,22 +417,24 @@
             pltpu.VMEM((slabs, SUB, LANES), F32),
             pltpu.VMEM((slabs, taps + 1, LANES), F32),
             pltpu.VMEM((LANES, LANES), F32),
-            pltpu.VMEM((chips, rows, width), BF16),
-            pltpu.VMEM((chips, rows, width), BF16),
-            pltpu.VMEM((chips, rows, width), BF16),
-            pltpu.VMEM((chips, rows, width), BF16),
+            pltpu.VMEM((parts, chips, rows, part), BF16),
+            pltpu.VMEM((parts, chips, rows, part), BF16),
+            pltpu.VMEM((parts, chips, rows, part), BF16),
+            pltpu.VMEM((parts, chips, rows, part), BF16),
             pltpu.VMEM((rows, width), F32),
-            pltpu.VMEM((rows, width), BF16),
-            pltpu.VMEM((n_dp, sub, width), BF16),
-            pltpu.VMEM((rows, width), BF16),
+            pltpu.VMEM((parts, rows, part), BF16),
+            pltpu.VMEM((parts, n_dp, sub, part), BF16),
+            pltpu.VMEM((parts, rows, part), BF16),
             pltpu.VMEM((n_seq, taps + 1, LANES), F32),
             pltpu.VMEM((taps + 1, LANES), F32),
             pltpu.VMEM((n_dp, taps + 1, LANES), F32),
-            sem(3), sem(4), sem(4), sem(chips), sem(chips), sem(chips), sem(chips),
-            sem(n_dp), sem(n_dp), sem(n_dp), sem(n_dp), sem(n_seq), sem(n_seq), sem(n_dp), sem(n_dp),
+            sem(7), sem(4), sem(4),
+            sem(parts, chips), sem(parts, chips), sem(parts, chips), sem(parts, chips),
+            sem(parts, n_dp), sem(parts, n_dp), sem(parts, n_dp), sem(parts, n_dp),
+            sem(n_seq), sem(n_seq), sem(n_dp), sem(n_dp),
         ],
         compiler_params=pltpu.CompilerParams(
-            collective_id=0, has_side_effects=True, vmem_limit_bytes=48 << 20
+            collective_id=0, has_side_effects=True, vmem_limit_bytes=60 << 20
         ),
         name="fused",
     )(seg, kern, gain, hid, proj, cot)

time: 57.8 us -> 60 us (1.038)
  Pallas kernels: 46.9 us -> 49.8 us
  local copies, waits for them, and re-layouts: 9.9 us -> 9.2 us
    pallas_call x1, Pallas kernels: 46.9 us -> 49.8 us  [fused(): pl.pallas_call(functools.partial(fused_kernel, n_dp, n_seq, factor), out_...]
    unnamed x14 -> x6, local copies, waits for them, and re-layouts: 8.33 us -> 6.11 us
    slice x1, local copies, waits for them, and re-layouts: 0.69 us -> 1.53 us  [body(): tail[:, taps]]
    broadcast_in_dim x1, local copies, waits for them, and re-layouts: 0.1 us -> 0.78 us  [body(): seg = jnp.broadcast_to(seg_wide[:, None], (length + 2 * HALO, LANES))]
where the time goes in v3:
time: 60 us; the launch traced here: 59.6 us
  Pallas kernels  49.8 us (83%)
  local copies, waits for them, and re-layouts  9.2 us (15%)
  between operations  0.65 us (1%)
    pallas_call x1, Pallas kernels, fused(): pl.pallas_call(functools.partial(fused_kernel, n_dp, n_seq, factor), out_...  49.8 us
    unnamed x6, local copies, waits for them, and re-layouts  6.11 us
    slice x1, local copies, waits for them, and re-layouts, body(): tail[:, taps]  1.53 us

profile of v3, /device:TPU:0, one launch (start us, length us, event | category | flops | bytes accessed | tf_op | source)
XLA Modules:
  0.0 59.6 jit_solution(11974946430333496065)
XLA Ops:
  0.6 0.8 %pad_dynamic-slice_fusion = s32[320]{0:T(512)S(1)} fusion(s32[]{:T(128)S(6)} %select_n.3, s32[2048]{0:T(1024)} %bitcast.12), kind=kLoop, calls=%fused_computation.1 | loop fusion | bytes 9476 | tf_op jit(solution)/shard_map/dynamic_slice | solution.py:449
  1.4 0.8 %broadcast_in_dim.15.seg = s32[320,128]{1,0:T(8,128)} broadcast(s32[320]{0:T(512)S(1)} %pad_dynamic-slice_fusion), dimensions={0} | broadcast | bytes 165120 | tf_op jit(solution)/shard_map/broadcast_in_dim | solution.py:450
  2.2 49.8 %fused.1 = (bf16[256,1024]{1,0:T(8,128)(2,1)}, bf16[256,1024]{1,0:T(8,128)(2,1)}, f32[128,1024]{1,0:T(8,128)}, f32[128,128]{1,0:T(8,128)}) custom-call(s32[320,128]{1,0:T(8,128)} %broadcast_in_dim.15.seg, f32[31,1024]{1,0:T(8,128)} %kern_in.1, f32[1,1024]{1,0:T(1,128)} %bitcast.13, bf16[256,1024]{1,0:T(8,128)(2,1)} %bitcast.9, bf16[1024,1024]{1,0:T(8,128)(2,1)} %proj_in.1, ...), custom_call_target="tpu_custom_call" | custom-call | tf_op jit(solution)/shard_map/fused/pallas_call | solution.py:387
  52.0 0.0 copy-start
  52.0 1.6 %copy.12 = f32[128,31]{0,1:T(8,128)} copy(f32[128,31]{1,0:T(8,128)} %bitcast.11) | data formatting | bytes 31744
  53.6 1.5 %slice_reduce_fusion = f32[128]{0:T(128)} fusion(f32[128,128]{1,0:T(8,128)} %get-tuple-element.12), kind=kLoop, calls=%fused_computation | loop fusion | bytes 1024 | tf_op jit(solution)/shard_map/slice | solution.py:456
  55.1 1.9 %copy.16 = bf16[1,256,1024]{2,1,0:T(8,128)(2,1)} copy(bf16[1,256,1024]{2,1,0:T(8,128)(2,1)} %bitcast.8) | data formatting | bytes 1048576
  57.0 1.9 %copy.17 = bf16[1,256,1024]{2,1,0:T(8,128)(2,1)} copy(bf16[1,256,1024]{2,1,0:T(8,128)(2,1)} %bitcast.7) | data formatting | bytes 1048576
  58.8 0.0 copy-done
  58.8 0.8 %copy.18 = f32[128,1024]{1,0:T(8,128)} copy(f32[128,1024]{1,0:T(8,128)S(1)} %copy-done) | data formatting | bytes 1048576
Async XLA Ops:
  52.0 6.9 %copy-start = (f32[128,1024]{1,0:T(8,128)S(1)}, f32[128,1024]{1,0:T(8,128)}, u32[]{:S(2)}) copy-start(f32[128,1024]{1,0:T(8,128)} %get-tuple-element.30) | copy-start | bytes 1572868
